TPU v7x, 32 devices: a whole 2x2x4 slice. The times are simulated.
32 devices in a mesh: batch: 2 (over y), row: 16 (over z, x, core).
Axes of the slice: x: 2, y: 2, z: 4, core: 2. Of those that a mesh axis runs over, the one named last changes fastest.
Arguments:
- tensor: float32 [128, 3, 4, 128, 128], P(('batch', 'row')), parts along dimension 0, may hold values from -0.5 to 0.5
- density: float32 [128, 5, 128, 128], P(('batch', 'row')), parts along dimension 0, as said below
- metric: float32 [8, 4], P('batch'), parts along dimension 0, as said below
- offsets: int32 [128, 3], P('batch'), parts along dimension 0, may hold values from -2 to 2, as said below
- counts: int32 [128], P('batch'), parts along dimension 0, may hold values from 1 to 3, as said below
Outputs:
- exchange: float32 [128, 5, 128, 128], P(('batch', 'row')), parts along dimension 0
There are 2 independent parts, one for each index of `batch`. A program takes and returns all parts, laid end to end along the dimension named above; each array names one. Nothing has to cross between parts.
Inputs may be any that keep to these rules, and one draw needn't show every extreme that they name: Each row holds 3 different offsets. Slots from counts[m] on are padding. density is symmetric: density[l, k] is the transpose of density[l + k - 2, 4 - k], block indices modulo 64. metric is symmetric.
All inputs are finite; a program needn't handle non-finite values.
Results may differ from a plain program's by a relative error of at most 0.0003.
Values sent between devices are 32-bit elements; how exact they have to be, the bound alone decides.
A program may use at most 128 MiB of HBM per device.

v0:
```python
import functools

import jax
import jax.numpy as jnp
from jax import lax
from jax.experimental import pallas as pl
from jax.experimental.pallas import tpu as pltpu
from jax.sharding import PartitionSpec as P

MESH = pl.DeviceIdType.MESH
F32 = jnp.float32
BF16 = jnp.bfloat16
RADIUS = 2
WIDTH = 2 * RADIUS + 1
BLOCKS = 4
SLOTS = 3
AUX = 4
B = 128
ZERO = 8 * WIDTH
COLS = 13


def split(x):
    hi = x.astype(BF16)
    return hi, (x - hi.astype(F32)).astype(BF16)


def dot(a, b):
    return jnp.dot(a, b, preferred_element_type=F32)


def dot_t(a, b):
    return lax.dot_general(a, b, (((1,), (1,)), ((), ())), preferred_element_type=F32)


def kernel(
    ring,
    ten_hbm,
    den_hbm,
    metric,
    offsets,
    counts,
    out,
    ten,
    den,
    den_l3,
    den_l2,
    den_r0,
    den_r1,
    ten_l,
    ten_r,
    d_hi,
    d_lo,
    v_hi,
    v_lo,
    u_hi,
    u_lo,
    e_hi,
    e_lo,
    to_right,
    to_left,
    from_left,
    from_right,
    local_sem,
    send_sem,
    recv_sem,
):
    me = lax.axis_index("row")
    right = lax.rem(me + 1, ring)
    left = lax.rem(me + ring - 1, ring)
    total = ring * BLOCKS
    first = me * BLOCKS

    own_ten = pltpu.make_async_copy(ten_hbm, ten, local_sem.at[0])
    own_den = pltpu.make_async_copy(den_hbm, den, local_sem.at[1])
    own_den.start()
    own_ten.start()

    barrier = pltpu.get_barrier_semaphore()
    for side in (left, right):
        pl.semaphore_signal(barrier, inc=1, device_id={"row": side}, device_id_type=MESH)
    pl.semaphore_wait(barrier, 2)

    def remote(src, dst, number, side):
        return pltpu.make_async_remote_copy(
            src_ref=src,
            dst_ref=dst,
            send_sem=send_sem.at[number],
            recv_sem=recv_sem.at[number],
            device_id={"row": side},
            device_id_type=MESH,
        )

    den_moves = [
        remote(den_hbm.at[3, 0:3], den_l3, 0, right),
        remote(den_hbm.at[0, 2:5], den_r0, 1, left),
        remote(den_hbm.at[2, 2], den_l2, 2, right),
        remote(den_hbm.at[1, 2:4], den_r1, 3, left),
    ]
    ten_moves = [
        remote(ten_hbm.at[0], ten_r, 4, left),
        remote(ten_hbm.at[3], ten_l, 5, right),
    ]
    for move in den_moves + ten_moves:
        move.start()

    def block_offset(n, s):
        return offsets[lax.rem(first + n + total, total), s]

    def block_live(n, s):
        return jnp.where(s < counts[lax.rem(first + n + total, total)], 1.0, 0.0).astype(F32)

    def put(i, k, block):
        hi, lo = split(block)
        d_hi[(i + RADIUS) * WIDTH + k] = hi
        d_lo[(i + RADIUS) * WIDTH + k] = lo

    own_den.wait()
    for number in (0, 1, 7 * WIDTH + 4, ZERO):
        d_hi[number] = jnp.zeros((B, B), BF16)
        d_lo[number] = jnp.zeros((B, B), BF16)

    def own_rows(step, carry):
        hi, lo = split(den[step])
        at = pl.ds((step + RADIUS) * WIDTH, WIDTH)
        d_hi[at] = hi
        d_lo[at] = lo
        return carry

    lax.fori_loop(0, BLOCKS, own_rows, 0)
    for i, j in ((-1, 0), (-1, 1), (-2, 0), (4, 2), (4, 3), (5, 3)):
        put(i, j - i + RADIUS, den[j, i - j + RADIUS].T)

    own_ten.wait()

    def prepare(m, carry):
        for s in range(SLOTS):
            live = block_live(m, s)
            parts = [ten[m, s, p] * live for p in range(AUX)]
            for q in range(AUX):
                hi, lo = split(parts[q])
                u_hi[m, s, :, q * B : (q + 1) * B] = hi
                u_lo[m, s, :, q * B : (q + 1) * B] = lo
                mixed = metric[q, 0] * parts[0]
                for p in range(1, AUX):
                    mixed = mixed + metric[q, p] * parts[p]
                hi, lo = split(mixed)
                v_hi[m, q * B : (q + 1) * B, s * B : (s + 1) * B] = hi
                v_lo[m, q * B : (q + 1) * B, s * B : (s + 1) * B] = lo
        return carry

    lax.fori_loop(0, BLOCKS, prepare, 0)

    for move in den_moves:
        move.wait_recv()
    for k in range(3):
        put(-1, k, den_l3[k])
        put(4, k + 2, den_r0[k])
    put(-2, 2, den_l2[...])
    put(-2, 3, den_l3[1].T)
    put(5, 1, den_r0[1].T)
    put(5, 2, den_r1[0])
    put(5, 3, den_r1[1])

    def half(m, o):
        rows_hi, rows_lo = [], []
        for s in range(SLOTS):
            shift = block_offset(m, s)
            pair_hi, pair_lo = [], []
            for step in (0, 1):
                k = o + step - shift + RADIUS
                at = jnp.where(
                    jnp.logical_and(k >= 0, k < WIDTH),
                    (m + shift + RADIUS) * WIDTH + k,
                    ZERO,
                )
                pair_hi.append(d_hi[at])
                pair_lo.append(d_lo[at])
            rows_hi.append(jnp.concatenate(pair_hi, axis=1))
            rows_lo.append(jnp.concatenate(pair_lo, axis=1))
        right_hi = jnp.concatenate(rows_hi, axis=0)
        right_lo = jnp.concatenate(rows_lo, axis=0)
        left_hi = v_hi[m]
        result = dot(left_hi, right_hi) + (dot(left_hi, right_lo) + dot(v_lo[m], right_hi))
        rows = pl.ds(pl.multiple_of(m * B, B), B)
        for step in (0, 1):
            for q in range(AUX):
                hi, lo = split(result[q * B : (q + 1) * B, step * B : (step + 1) * B])
                e_hi[m + o + step + 4, rows, q * B : (q + 1) * B] = hi
                e_lo[m + o + step + 4, rows, q * B : (q + 1) * B] = lo

    def all_halves(number, carry):
        half(number // 4, (number % 4) * 2 - 2)
        return carry

    lax.fori_loop(0, 4 * BLOCKS, all_halves, 0)
    half(1, -4)

    def close(n, start, stop, part_hi, part_lo):
        result = jnp.zeros(((stop - start) * B, B), F32)
        for s in range(SLOTS):
            at = n + block_offset(n, s) + 4
            left_hi = e_hi[at, start * B : stop * B, :]
            left_lo = e_lo[at, start * B : stop * B, :]
            right_hi, right_lo = part_hi(s), part_lo(s)
            result = result + (
                dot_t(left_hi, right_hi) + (dot_t(left_hi, right_lo) + dot_t(left_lo, right_hi))
            )
        return [result[i * B : (i + 1) * B] for i in range(stop - start)]

    for n in range(BLOCKS):
        start = max(0, n - RADIUS)
        found = close(n, start, n + 1, lambda s: u_hi[n, s], lambda s: u_lo[n, s])
        for m in range(start, n + 1):
            block = found[m - start]
            out[m, n - m + RADIUS] = block
            if m < n:
                out[n, m - n + RADIUS] = block.T

    def arrived(buffer, n):
        def one(s):
            live = block_live(n, s)
            pieces = [split(buffer[s, q] * live) for q in range(AUX)]
            return [jnp.concatenate([piece[i] for piece in pieces], axis=1) for i in (0, 1)]

        both = [one(s) for s in range(SLOTS)]
        return (lambda s: both[s][0]), (lambda s: both[s][1])

    answer_right = remote(to_right, from_left, 6, right)
    answer_left = remote(to_left, from_right, 7, left)

    ten_moves[0].wait_recv()
    found = close(4, 2, 4, *arrived(ten_r, 4))
    for i in (0, 1):
        to_right[i] = found[i].T
    answer_right.start()
    for i in (0, 1):
        out[2 + i, 4 - i] = found[i]

    ten_moves[1].wait_recv()
    found = close(-1, 1, 2, *arrived(ten_l, -1))
    to_left[...] = found[0].T
    answer_left.start()
    out[1, 0] = found[0]

    answer_right.wait_recv()
    out[0, 0] = from_left[0]
    out[0, 1] = from_left[1]
    answer_left.wait_recv()
    out[3, 4] = from_right[...]
    for move in den_moves + ten_moves + [answer_right, answer_left]:
        move.wait_send()


def body(tensor, density, metric, offsets, counts):
    ring = lax.axis_size("row")
    any_space = pl.BlockSpec(memory_space=pl.ANY)
    smem = pl.BlockSpec(memory_space=pltpu.SMEM)
    return pl.pallas_call(
        functools.partial(kernel, ring),
        out_shape=jax.ShapeDtypeStruct(density.shape, F32),
        in_specs=[any_space, any_space, smem, smem, smem],
        out_specs=pl.BlockSpec(memory_space=pltpu.VMEM),
        scratch_shapes=[
            pltpu.VMEM((BLOCKS, SLOTS, AUX, B, B), F32),
            pltpu.VMEM((BLOCKS, WIDTH, B, B), F32),
            pltpu.VMEM((3, B, B), F32),
            pltpu.VMEM((B, B), F32),
            pltpu.VMEM((3, B, B), F32),
            pltpu.VMEM((2, B, B), F32),
            pltpu.VMEM((SLOTS, AUX, B, B), F32),
            pltpu.VMEM((SLOTS, AUX, B, B), F32),
            pltpu.VMEM((ZERO + 1, B, B), BF16),
            pltpu.VMEM((ZERO + 1, B, B), BF16),
            pltpu.VMEM((BLOCKS, AUX * B, SLOTS * B), BF16),
            pltpu.VMEM((BLOCKS, AUX * B, SLOTS * B), BF16),
            pltpu.VMEM((BLOCKS, SLOTS, B, AUX * B), BF16),
            pltpu.VMEM((BLOCKS, SLOTS, B, AUX * B), BF16),
            pltpu.VMEM((COLS, BLOCKS * B, AUX * B), BF16),
            pltpu.VMEM((COLS, BLOCKS * B, AUX * B), BF16),
            pltpu.VMEM((2, B, B), F32),
            pltpu.VMEM((B, B), F32),
            pltpu.VMEM((2, B, B), F32),
            pltpu.VMEM((B, B), F32),
            pltpu.SemaphoreType.DMA((2,)),
            pltpu.SemaphoreType.DMA((8,)),
            pltpu.SemaphoreType.DMA((8,)),
        ],
        compiler_params=pltpu.CompilerParams(
            collective_id=0, has_side_effects=True, vmem_limit_bytes=48 * 1024 * 1024
        ),
        cost_estimate=pl.CostEstimate(flops=6 * 10**9, bytes_accessed=6 * 10**6, transcendentals=0),
    )(tensor, density, metric, offsets, counts)


def solution(mesh):
    return jax.shard_map(
        body,
        mesh=mesh,
        in_specs=(
            P(("batch", "row"), None, None, None, None),
            P(("batch", "row"), None, None, None),
            P("batch", None),
            P("batch", None),
            P("batch"),
        ),
        out_specs=P(("batch", "row"), None, None, None),
        check_vma=False,
    )
```

profile of v0, /device:TPU:1, one launch (start us, length us, event | category | flops | bytes accessed | tf_op | source)
XLA Modules:
  0.0 46.7 jit_solution(15466741642254935934)
XLA Ops:
  0.0 0.8 %copy.6.offsets = s32[64,3]{1,0:T(8,128)S(1)} copy(s32[64,3]{0,1:T(4,128)} %param.8) | data formatting | bytes 1536 | tf_op args[3]
  0.8 0.0 copy-start
  0.8 1.9 %copy-done = f32[4,3,4,128,128]{4,3,2,1,0:T(8,128)S(1)} copy-done((f32[4,3,4,128,128]{4,3,2,1,0:T(8,128)S(1)}, f32[4,3,4,128,128]{4,3,2,1,0:T(8,128)}, u32[]{:S(2)}) %copy-start) | copy-done | bytes 3145752
  2.7 0.0 copy-start.1
  2.7 1.3 %copy-done.1 = f32[4,5,128,128]{3,2,1,0:T(8,128)S(1)} copy-done((f32[4,5,128,128]{3,2,1,0:T(8,128)S(1)}, f32[4,5,128,128]{3,2,1,0:T(8,128)}, u32[]{:S(2)}) %copy-start.1) | copy-done | bytes 1310744
  4.0 0.0 copy-start.2
  4.0 0.7 %copy-done.2 = f32[4,4]{1,0:T(4,128)S(1)} copy-done((f32[4,4]{1,0:T(4,128)S(1)}, f32[4,4]{1,0:T(4,128)}, u32[]{:S(2)}) %copy-start.2) | copy-done | bytes 88
  4.7 0.0 copy-start.3
  4.7 0.7 %copy-done.3 = s32[64]{0:T(128)S(1)} copy-done((s32[64]{0:T(128)S(1)}, s32[64]{0:T(128)}, u32[]{:S(2)}) %copy-start.3) | copy-done | bytes 280
  5.3 40.3 %shard_map.55 = f32[4,5,128,128]{3,2,1,0:T(8,128)S(1)} custom-call(f32[4,3,4,128,128]{4,3,2,1,0:T(8,128)S(1)} %copy-done, f32[4,5,128,128]{3,2,1,0:T(8,128)S(1)} %copy-done.1, f32[4,4]{1,0:T(4,128)S(1)} %copy-done.2, s32[64,3]{1,0:T(8,128)S(1)} %copy.6.offsets, s32[64]{0:T(128)S(1)} %copy-done.3), custom_call_target="tpu_custom_call" | custom-call | flops 6000000000 | bytes 6000000 | tf_op jit(solution)/shard_map/pallas_call | solution.py:259
  45.6 1.1 %copy.8 = f32[4,5,128,128]{3,2,1,0:T(8,128)} copy(f32[4,5,128,128]{3,2,1,0:T(8,128)S(1)} %shard_map.55) | data formatting | bytes 2621440
Async XLA Ops:
  0.8 1.9 %copy-start = (f32[4,3,4,128,128]{4,3,2,1,0:T(8,128)S(1)}, f32[4,3,4,128,128]{4,3,2,1,0:T(8,128)}, u32[]{:S(2)}) copy-start(f32[4,3,4,128,128]{4,3,2,1,0:T(8,128)} %ten_hbm.1) | copy-start | bytes 9437188
  2.7 1.3 %copy-start.1 = (f32[4,5,128,128]{3,2,1,0:T(8,128)S(1)}, f32[4,5,128,128]{3,2,1,0:T(8,128)}, u32[]{:S(2)}) copy-start(f32[4,5,128,128]{3,2,1,0:T(8,128)} %den_hbm.1) | copy-start | bytes 3932164
  4.0 0.7 %copy-start.2 = (f32[4,4]{1,0:T(4,128)S(1)}, f32[4,4]{1,0:T(4,128)}, u32[]{:S(2)}) copy-start(f32[4,4]{1,0:T(4,128)} %metric.1) | copy-start | bytes 196
  4.7 0.7 %copy-start.3 = (s32[64]{0:T(128)S(1)}, s32[64]{0:T(128)}, u32[]{:S(2)}) copy-start(s32[64]{0:T(128)} %counts.1) | copy-start | bytes 772
where the time goes:
time: 46.9 us; the launch traced here: 46.7 us
  Pallas kernels  40.3 us (86%)
  local copies, waits for them, and re-layouts  6.37 us (14%)
    pallas_call x1, Pallas kernels, body(): pl.pallas_call(functools.partial(kernel, ring), out_shape=jax.ShapeDtypeS...  40.3 us
    unnamed x10, local copies, waits for them, and re-layouts  6.37 us

commit v1 on v0

--- a/solution.py
+++ b/solution.py
@@ -17,6 +17,8 @@
 AUX = 4
 B = 128
 ZERO = 8 * WIDTH
+CHUNKS = 2
+ROWS = B // CHUNKS
 COLS = 13
 
 
@@ -37,10 +39,13 @@
     ring,
     ten_hbm,
     den_hbm,
+    metric_hbm,
+    offsets_hbm,
+    counts_hbm,
+    out,
     metric,
     offsets,
     counts,
-    out,
     ten,
     den,
     den_l3,
@@ -51,8 +56,7 @@
     ten_r,
     d_hi,
     d_lo,
-    v_hi,
-    v_lo,
+    v,
     u_hi,
     u_lo,
     e_hi,
@@ -73,6 +77,14 @@
 
     own_ten = pltpu.make_async_copy(ten_hbm, ten, local_sem.at[0])
     own_den = pltpu.make_async_copy(den_hbm, den, local_sem.at[1])
+    small = [
+        pltpu.make_async_copy(src, dst, local_sem.at[2 + i])
+        for i, (src, dst) in enumerate(
+            ((metric_hbm, metric), (offsets_hbm, offsets), (counts_hbm, counts))
+        )
+    ]
+    for move in small:
+        move.start()
     own_den.start()
     own_ten.start()
 
@@ -97,15 +109,29 @@
         remote(den_hbm.at[2, 2], den_l2, 2, right),
         remote(den_hbm.at[1, 2:4], den_r1, 3, left),
     ]
+    rows_of = [pl.ds(c * ROWS, ROWS) for c in range(CHUNKS)]
     ten_moves = [
-        remote(ten_hbm.at[0], ten_r, 4, left),
-        remote(ten_hbm.at[3], ten_l, 5, right),
+        [
+            remote(ten_hbm.at[0, :, :, rows_of[c]], ten_r.at[:, :, rows_of[c]], 4 + 4 * c, left),
+            remote(ten_hbm.at[3, :, :, rows_of[c]], ten_l.at[:, :, rows_of[c]], 5 + 4 * c, right),
+        ]
+        for c in range(CHUNKS)
     ]
-    for move in den_moves + ten_moves:
+    for move in den_moves:
         move.start()
+    for pair in ten_moves:
+        for move in pair:
+            move.start()
+    answers = [
+        [
+            remote(to_right.at[:, rows_of[c]], from_left.at[:, rows_of[c]], 6 + 4 * c, right),
+            remote(to_left.at[rows_of[c]], from_right.at[rows_of[c]], 7 + 4 * c, left),
+        ]
+        for c in range(CHUNKS)
+    ]
 
     def block_offset(n, s):
-        return offsets[lax.rem(first + n + total, total), s]
+        return offsets[s, lax.rem(first + n + total, total)]
 
     def block_live(n, s):
         return jnp.where(s < counts[lax.rem(first + n + total, total)], 1.0, 0.0).astype(F32)
@@ -116,7 +142,7 @@
         d_lo[(i + RADIUS) * WIDTH + k] = lo
 
     own_den.wait()
-    for number in (0, 1, 7 * WIDTH + 4, ZERO):
+    for number in (0, 1, 2, 3, 5, 6, 7, 32, 33, 34, 36, 37, 38, 39, ZERO):
         d_hi[number] = jnp.zeros((B, B), BF16)
         d_lo[number] = jnp.zeros((B, B), BF16)
 
@@ -132,6 +158,8 @@
         put(i, j - i + RADIUS, den[j, i - j + RADIUS].T)
 
     own_ten.wait()
+    for move in small:
+        move.wait()
 
     def prepare(m, carry):
         for s in range(SLOTS):
@@ -145,22 +173,12 @@
                 for p in range(1, AUX):
                     mixed = mixed + metric[q, p] * parts[p]
                 hi, lo = split(mixed)
-                v_hi[m, q * B : (q + 1) * B, s * B : (s + 1) * B] = hi
-                v_lo[m, q * B : (q + 1) * B, s * B : (s + 1) * B] = lo
+                v[m, s, 0, q * B : (q + 1) * B] = hi
+                v[m, s, 1, q * B : (q + 1) * B] = lo
+        v[m, SLOTS] = jnp.zeros((2, AUX * B, B), BF16)
         return carry
 
     lax.fori_loop(0, BLOCKS, prepare, 0)
-
-    for move in den_moves:
-        move.wait_recv()
-    for k in range(3):
-        put(-1, k, den_l3[k])
-        put(4, k + 2, den_r0[k])
-    put(-2, 2, den_l2[...])
-    put(-2, 3, den_l3[1].T)
-    put(5, 1, den_r0[1].T)
-    put(5, 2, den_r1[0])
-    put(5, 3, den_r1[1])
 
     def half(m, o):
         rows_hi, rows_lo = [], []
@@ -178,10 +196,12 @@
                 pair_lo.append(d_lo[at])
             rows_hi.append(jnp.concatenate(pair_hi, axis=1))
             rows_lo.append(jnp.concatenate(pair_lo, axis=1))
-        right_hi = jnp.concatenate(rows_hi, axis=0)
-        right_lo = jnp.concatenate(rows_lo, axis=0)
-        left_hi = v_hi[m]
-        result = dot(left_hi, right_hi) + (dot(left_hi, right_lo) + dot(v_lo[m], right_hi))
+        left_hi = [v[m, s, 0] for s in range(SLOTS)]
+        left_lo = [v[m, s, 1] for s in range(SLOTS)]
+        result = dot(
+            jnp.concatenate(left_hi + left_hi + left_lo, axis=1),
+            jnp.concatenate(rows_hi + rows_lo + rows_hi, axis=0),
+        )
         rows = pl.ds(pl.multiple_of(m * B, B), B)
         for step in (0, 1):
             for q in range(AUX):
@@ -195,6 +215,42 @@
 
     lax.fori_loop(0, 4 * BLOCKS, all_halves, 0)
     half(1, -4)
+
+    def slot_at(m, shift):
+        at = SLOTS
+        for s in range(SLOTS):
+            at = jnp.where(block_offset(m, s) == shift, s, at)
+        return at
+
+    def add_half(m, shifts, columns, blocks):
+        ats = [slot_at(m, shift) for shift in shifts]
+        left_hi = [v[m, at, 0] for at in ats]
+        left_lo = [v[m, at, 1] for at in ats]
+        rows_hi = [jnp.concatenate([b[0] for b in row], axis=1) for row in blocks]
+        rows_lo = [jnp.concatenate([b[1] for b in row], axis=1) for row in blocks]
+        result = dot(
+            jnp.concatenate(left_hi + left_hi + left_lo, axis=1),
+            jnp.concatenate(rows_hi + rows_lo + rows_hi, axis=0),
+        )
+        rows = slice(m * B, (m + 1) * B)
+        for step, j in enumerate(columns):
+            for q in range(AUX):
+                lanes = slice(q * B, (q + 1) * B)
+                old = e_hi[j + 4, rows, lanes].astype(F32) + e_lo[j + 4, rows, lanes].astype(F32)
+                hi, lo = split(old + result[lanes, step * B : (step + 1) * B])
+                e_hi[j + 4, rows, lanes] = hi
+                e_lo[j + 4, rows, lanes] = lo
+
+    for move in den_moves:
+        move.wait_recv()
+    row_l1 = [split(den_l3[k]) for k in range(3)]
+    row_l2 = [split(den_l2[...]), split(den_l3[1].T)]
+    add_half(0, (-1, -2), (-2, -1), [row_l1[1:], row_l2])
+    add_half(1, (-2,), (-3, -2, -1), [row_l1])
+    row_r0 = [split(den_r0[k]) for k in range(3)]
+    row_r1 = [split(den_r0[1].T), split(den_r1[0]), split(den_r1[1])]
+    add_half(2, (2,), (4, 5, 6), [row_r0])
+    add_half(3, (1, 2), (4, 5, 6), [row_r0, row_r1])
 
     def close(n, start, stop, part_hi, part_lo):
         result = jnp.zeros(((stop - start) * B, B), F32)
@@ -217,51 +273,63 @@
             if m < n:
                 out[n, m - n + RADIUS] = block.T
 
-    def arrived(buffer, n):
-        def one(s):
+    def close_arrived(buffer, n, start, stop, rows):
+        result = jnp.zeros((ROWS, (stop - start) * B), F32)
+        for s in range(SLOTS):
             live = block_live(n, s)
-            pieces = [split(buffer[s, q] * live) for q in range(AUX)]
-            return [jnp.concatenate([piece[i] for piece in pieces], axis=1) for i in (0, 1)]
-
-        both = [one(s) for s in range(SLOTS)]
-        return (lambda s: both[s][0]), (lambda s: both[s][1])
-
-    answer_right = remote(to_right, from_left, 6, right)
-    answer_left = remote(to_left, from_right, 7, left)
-
-    ten_moves[0].wait_recv()
-    found = close(4, 2, 4, *arrived(ten_r, 4))
+            pieces = [split(buffer[s, q, rows] * live) for q in range(AUX)]
+            left_hi, left_lo = [
+                jnp.concatenate([piece[i] for piece in pieces], axis=1) for i in (0, 1)
+            ]
+            at = n + block_offset(n, s) + 4
+            right_hi = e_hi[at, start * B : stop * B, :]
+            right_lo = e_lo[at, start * B : stop * B, :]
+            result = result + (
+                dot_t(left_hi, right_hi) + (dot_t(left_hi, right_lo) + dot_t(left_lo, right_hi))
+            )
+        return [result[:, i * B : (i + 1) * B] for i in range(stop - start)]
+
+    for c in range(CHUNKS):
+        rows = slice(c * ROWS, (c + 1) * ROWS)
+        ten_moves[c][0].wait_recv()
+        found = close_arrived(ten_r, 4, 2, 4, rows)
+        for i in (0, 1):
+            to_right[i, rows] = found[i]
+        answers[c][0].start()
+        ten_moves[c][1].wait_recv()
+        (found,) = close_arrived(ten_l, -1, 1, 2, rows)
+        to_left[rows] = found
+        answers[c][1].start()
+
     for i in (0, 1):
-        to_right[i] = found[i].T
-    answer_right.start()
-    for i in (0, 1):
-        out[2 + i, 4 - i] = found[i]
-
-    ten_moves[1].wait_recv()
-    found = close(-1, 1, 2, *arrived(ten_l, -1))
-    to_left[...] = found[0].T
-    answer_left.start()
-    out[1, 0] = found[0]
-
-    answer_right.wait_recv()
+        out[2 + i, 4 - i] = to_right[i].T
+    out[1, 0] = to_left[...].T
+
+    for pair in answers:
+        for move in pair:
+            move.wait_recv()
     out[0, 0] = from_left[0]
     out[0, 1] = from_left[1]
-    answer_left.wait_recv()
     out[3, 4] = from_right[...]
-    for move in den_moves + ten_moves + [answer_right, answer_left]:
+    for move in den_moves:
         move.wait_send()
+    for pair in ten_moves + answers:
+        for move in pair:
+            move.wait_send()
 
 
 def body(tensor, density, metric, offsets, counts):
     ring = lax.axis_size("row")
-    any_space = pl.BlockSpec(memory_space=pl.ANY)
-    smem = pl.BlockSpec(memory_space=pltpu.SMEM)
+    hbm = pl.BlockSpec(memory_space=pltpu.HBM)
     return pl.pallas_call(
         functools.partial(kernel, ring),
         out_shape=jax.ShapeDtypeStruct(density.shape, F32),
-        in_specs=[any_space, any_space, smem, smem, smem],
+        in_specs=[hbm] * 5,
         out_specs=pl.BlockSpec(memory_space=pltpu.VMEM),
         scratch_shapes=[
+            pltpu.SMEM(metric.shape, F32),
+            pltpu.SMEM(offsets.shape[::-1], jnp.int32),
+            pltpu.SMEM(counts.shape, jnp.int32),
             pltpu.VMEM((BLOCKS, SLOTS, AUX, B, B), F32),
             pltpu.VMEM((BLOCKS, WIDTH, B, B), F32),
             pltpu.VMEM((3, B, B), F32),
@@ -272,8 +340,7 @@
             pltpu.VMEM((SLOTS, AUX, B, B), F32),
             pltpu.VMEM((ZERO + 1, B, B), BF16),
             pltpu.VMEM((ZERO + 1, B, B), BF16),
-            pltpu.VMEM((BLOCKS, AUX * B, SLOTS * B), BF16),
-            pltpu.VMEM((BLOCKS, AUX * B, SLOTS * B), BF16),
+            pltpu.VMEM((BLOCKS, SLOTS + 1, 2, AUX * B, B), BF16),
             pltpu.VMEM((BLOCKS, SLOTS, B, AUX * B), BF16),
             pltpu.VMEM((BLOCKS, SLOTS, B, AUX * B), BF16),
             pltpu.VMEM((COLS, BLOCKS * B, AUX * B), BF16),
@@ -282,15 +349,15 @@
             pltpu.VMEM((B, B), F32),
             pltpu.VMEM((2, B, B), F32),
             pltpu.VMEM((B, B), F32),
-            pltpu.SemaphoreType.DMA((2,)),
-            pltpu.SemaphoreType.DMA((8,)),
-            pltpu.SemaphoreType.DMA((8,)),
+            pltpu.SemaphoreType.DMA((5,)),
+            pltpu.SemaphoreType.DMA((4 + 4 * CHUNKS,)),
+            pltpu.SemaphoreType.DMA((4 + 4 * CHUNKS,)),
         ],
         compiler_params=pltpu.CompilerParams(
-            collective_id=0, has_side_effects=True, vmem_limit_bytes=48 * 1024 * 1024
+            collective_id=0, has_side_effects=True, vmem_limit_bytes=57 * 1024 * 1024
         ),
         cost_estimate=pl.CostEstimate(flops=6 * 10**9, bytes_accessed=6 * 10**6, transcendentals=0),
-    )(tensor, density, metric, offsets, counts)
+    )(tensor, density, metric, offsets.T, counts)
 
 
 def solution(mesh):

time: 46.9 us -> 36 us (0.77)
  Pallas kernels: 40.3 us -> 33.4 us
  local copies, waits for them, and re-layouts: 6.37 us -> 2.5 us
    pallas_call x1, Pallas kernels: 40.3 us -> 33.4 us  [body(): pl.pallas_call(functools.partial(kernel, ring), out_shape=jax.ShapeDtypeS...]
    unnamed x10 -> x1, local copies, waits for them, and re-layouts: 6.37 us -> 2.5 us
where the time goes in v1:
time: 36 us; the launch traced here: 35.9 us
  Pallas kernels  33.4 us (93%)
  local copies, waits for them, and re-layouts  2.5 us (7%)
    pallas_call x1, Pallas kernels, body(): pl.pallas_call(functools.partial(kernel, ring), out_shape=jax.ShapeDtypeS...  33.4 us
    unnamed x1, local copies, waits for them, and re-layouts  2.5 us

profile of v1, /device:TPU:1, one launch (start us, length us, event | category | flops | bytes accessed | tf_op | source)
XLA Modules:
  0.0 35.9 jit_solution(16285940850191614789)
XLA Ops:
  0.0 33.4 %shard_map.55 = f32[4,5,128,128]{3,2,1,0:T(8,128)} custom-call(f32[4,3,4,128,128]{4,3,2,1,0:T(8,128)} %ten_hbm.1, f32[4,5,128,128]{3,2,1,0:T(8,128)} %den_hbm.1, f32[4,4]{1,0:T(4,128)} %metric_hbm.1, s32[3,64]{1,0:T(4,128)} %bitcast.1, s32[64]{0:T(128)} %counts_hbm.1), custom_call_target="tpu_custom_call" | custom-call | flops 6000000000 | bytes 6000000 | tf_op jit(solution)/shard_map/pallas_call | solution.py:324
  33.4 2.5 %copy.7 = f32[4,5,128,128]{3,2,1,0:T(8,128)} copy(f32[4,5,128,128]{3,2,1,0:T(8,128)} %shard_map.55) | data formatting | bytes 2621440

commit v2 on v1

--- a/solution.py
+++ b/solution.py
@@ -52,6 +52,9 @@
     den_l2,
     den_r0,
     den_r1,
+    den_r2,
+    pack_right,
+    pack_left,
     ten_l,
     ten_r,
     d_hi,
@@ -104,10 +107,11 @@
         )
 
     den_moves = [
-        remote(den_hbm.at[3, 0:3], den_l3, 0, right),
-        remote(den_hbm.at[0, 2:5], den_r0, 1, left),
-        remote(den_hbm.at[2, 2], den_l2, 2, right),
-        remote(den_hbm.at[1, 2:4], den_r1, 3, left),
+        remote(den_hbm.at[3, 0:2], den_l3, 0, right),
+        remote(den_hbm.at[0, 3:5], den_r0, 1, left),
+        remote(pack_right, den_l2, 2, right),
+        remote(pack_left, den_r1, 3, left),
+        remote(den_hbm.at[1, 3], den_r2, 4 + 4 * CHUNKS, left),
     ]
     rows_of = [pl.ds(c * ROWS, ROWS) for c in range(CHUNKS)]
     ten_moves = [
@@ -117,8 +121,30 @@
         ]
         for c in range(CHUNKS)
     ]
-    for move in den_moves:
-        move.start()
+    for number in (0, 1, 4):
+        den_moves[number].start()
+
+    row_of = lax.broadcasted_iota(jnp.int32, (B, B), 0)
+    col_of = lax.broadcasted_iota(jnp.int32, (B, B), 1)
+
+    def pack(buffer, one, two):
+        buffer[0:B] = jnp.where(row_of >= col_of, one, two)
+        diagonal = jnp.sum(jnp.where(row_of == col_of, two, 0.0), axis=0, keepdims=True)
+        buffer[B : B + 8] = jnp.broadcast_to(diagonal, (8, B))
+
+    def unpack(buffer):
+        both = buffer[0:B]
+        turned = both.T
+        one = jnp.where(row_of >= col_of, both, turned)
+        diagonal = jnp.broadcast_to(buffer[B : B + 1], (B, B))
+        two = jnp.where(row_of < col_of, both, jnp.where(row_of > col_of, turned, diagonal))
+        return one, two
+
+    own_den.wait()
+    pack(pack_right, den[3, 2], den[2, 2])
+    pack(pack_left, den[0, 2], den[1, 2])
+    den_moves[2].start()
+    den_moves[3].start()
     for pair in ten_moves:
         for move in pair:
             move.start()
@@ -141,7 +167,6 @@
         d_hi[(i + RADIUS) * WIDTH + k] = hi
         d_lo[(i + RADIUS) * WIDTH + k] = lo
 
-    own_den.wait()
     for number in (0, 1, 2, 3, 5, 6, 7, 32, 33, 34, 36, 37, 38, 39, ZERO):
         d_hi[number] = jnp.zeros((B, B), BF16)
         d_lo[number] = jnp.zeros((B, B), BF16)
@@ -243,12 +268,14 @@
 
     for move in den_moves:
         move.wait_recv()
-    row_l1 = [split(den_l3[k]) for k in range(3)]
-    row_l2 = [split(den_l2[...]), split(den_l3[1].T)]
+    near, far = unpack(den_l2)
+    row_l1 = [split(den_l3[0]), split(den_l3[1]), split(near)]
+    row_l2 = [split(far), split(den_l3[1].T)]
     add_half(0, (-1, -2), (-2, -1), [row_l1[1:], row_l2])
     add_half(1, (-2,), (-3, -2, -1), [row_l1])
-    row_r0 = [split(den_r0[k]) for k in range(3)]
-    row_r1 = [split(den_r0[1].T), split(den_r1[0]), split(den_r1[1])]
+    near, far = unpack(den_r1)
+    row_r0 = [split(near), split(den_r0[0]), split(den_r0[1])]
+    row_r1 = [split(den_r0[0].T), split(far), split(den_r2[...])]
     add_half(2, (2,), (4, 5, 6), [row_r0])
     add_half(3, (1, 2), (4, 5, 6), [row_r0, row_r1])
 
@@ -332,10 +359,13 @@
             pltpu.SMEM(counts.shape, jnp.int32),
             pltpu.VMEM((BLOCKS, SLOTS, AUX, B, B), F32),
             pltpu.VMEM((BLOCKS, WIDTH, B, B), F32),
-            pltpu.VMEM((3, B, B), F32),
+            pltpu.VMEM((2, B, B), F32),
+            pltpu.VMEM((B + 8, B), F32),
+            pltpu.VMEM((2, B, B), F32),
+            pltpu.VMEM((B + 8, B), F32),
             pltpu.VMEM((B, B), F32),
-            pltpu.VMEM((3, B, B), F32),
-            pltpu.VMEM((2, B, B), F32),
+            pltpu.VMEM((B + 8, B), F32),
+            pltpu.VMEM((B + 8, B), F32),
             pltpu.VMEM((SLOTS, AUX, B, B), F32),
             pltpu.VMEM((SLOTS, AUX, B, B), F32),
             pltpu.VMEM((ZERO + 1, B, B), BF16),
@@ -350,8 +380,8 @@
             pltpu.VMEM((2, B, B), F32),
             pltpu.VMEM((B, B), F32),
             pltpu.SemaphoreType.DMA((5,)),
-            pltpu.SemaphoreType.DMA((4 + 4 * CHUNKS,)),
-            pltpu.SemaphoreType.DMA((4 + 4 * CHUNKS,)),
+            pltpu.SemaphoreType.DMA((5 + 4 * CHUNKS,)),
+            pltpu.SemaphoreType.DMA((5 + 4 * CHUNKS,)),
         ],
         compiler_params=pltpu.CompilerParams(
             collective_id=0, has_side_effects=True, vmem_limit_bytes=57 * 1024 * 1024

time: 36 us -> 34.4 us (0.956)
  Pallas kernels: 33.4 us -> 31.7 us
    pallas_call x1, Pallas kernels: 33.4 us -> 31.7 us  [body(): pl.pallas_call(functools.partial(kernel, ring), out_shape=jax.ShapeDtypeS...]
where the time goes in v2:
time: 34.4 us; the launch traced here: 34.2 us
  Pallas kernels  31.7 us (92%)
  local copies, waits for them, and re-layouts  2.5 us (7%)
    pallas_call x1, Pallas kernels, body(): pl.pallas_call(functools.partial(kernel, ring), out_shape=jax.ShapeDtypeS...  31.7 us
    unnamed x1, local copies, waits for them, and re-layouts  2.5 us

profile of v2, /device:TPU:1, one launch (start us, length us, event | category | flops | bytes accessed | tf_op | source)
XLA Modules:
  0.0 34.2 jit_solution(10119575619350866186)
XLA Ops:
  0.0 31.7 %shard_map.55 = f32[4,5,128,128]{3,2,1,0:T(8,128)} custom-call(f32[4,3,4,128,128]{4,3,2,1,0:T(8,128)} %ten_hbm.1, f32[4,5,128,128]{3,2,1,0:T(8,128)} %den_hbm.1, f32[4,4]{1,0:T(4,128)} %metric_hbm.1, s32[3,64]{1,0:T(4,128)} %bitcast.1, s32[64]{0:T(128)} %counts_hbm.1), custom_call_target="tpu_custom_call" | custom-call | flops 6000000000 | bytes 6000000 | tf_op jit(solution)/shard_map/pallas_call | solution.py:351
  31.7 2.5 %copy.7 = f32[4,5,128,128]{3,2,1,0:T(8,128)} copy(f32[4,5,128,128]{3,2,1,0:T(8,128)} %shard_map.55) | data formatting | bytes 2621440

commit v3 on v2

--- a/solution.py
+++ b/solution.py
@@ -42,6 +42,7 @@
     metric_hbm,
     offsets_hbm,
     counts_hbm,
+    out_hbm,
     out,
     metric,
     offsets,
@@ -71,6 +72,7 @@
     local_sem,
     send_sem,
     recv_sem,
+    out_sem,
 ):
     me = lax.axis_index("row")
     right = lax.rem(me + 1, ring)
@@ -316,6 +318,16 @@
             )
         return [result[:, i * B : (i + 1) * B] for i in range(stop - start)]
 
+    def leave(number, m, start, stop):
+        return pltpu.make_async_copy(
+            out.at[m, start:stop], out_hbm.at[m, start:stop], out_sem.at[number]
+        )
+
+    early = [leave(0, 0, 2, 5), leave(1, 1, 1, 5), leave(2, 2, 0, 4), leave(3, 3, 0, 3)]
+    late = [leave(4, 0, 0, 2), leave(5, 1, 0, 1), leave(6, 2, 4, 5), leave(7, 3, 3, 5)]
+    for move in early:
+        move.start()
+
     for c in range(CHUNKS):
         rows = slice(c * ROWS, (c + 1) * ROWS)
         ten_moves[c][0].wait_recv()
@@ -331,6 +343,8 @@
     for i in (0, 1):
         out[2 + i, 4 - i] = to_right[i].T
     out[1, 0] = to_left[...].T
+    late[1].start()
+    late[2].start()
 
     for pair in answers:
         for move in pair:
@@ -338,6 +352,10 @@
     out[0, 0] = from_left[0]
     out[0, 1] = from_left[1]
     out[3, 4] = from_right[...]
+    late[0].start()
+    late[3].start()
+    for move in early + late:
+        move.wait()
     for move in den_moves:
         move.wait_send()
     for pair in ten_moves + answers:
@@ -352,8 +370,9 @@
         functools.partial(kernel, ring),
         out_shape=jax.ShapeDtypeStruct(density.shape, F32),
         in_specs=[hbm] * 5,
-        out_specs=pl.BlockSpec(memory_space=pltpu.VMEM),
+        out_specs=hbm,
         scratch_shapes=[
+            pltpu.VMEM(density.shape, F32),
             pltpu.SMEM(metric.shape, F32),
             pltpu.SMEM(offsets.shape[::-1], jnp.int32),
             pltpu.SMEM(counts.shape, jnp.int32),
@@ -382,6 +401,7 @@
             pltpu.SemaphoreType.DMA((5,)),
             pltpu.SemaphoreType.DMA((5 + 4 * CHUNKS,)),
             pltpu.SemaphoreType.DMA((5 + 4 * CHUNKS,)),
+            pltpu.SemaphoreType.DMA((8,)),
         ],
         compiler_params=pltpu.CompilerParams(
             collective_id=0, has_side_effects=True, vmem_limit_bytes=57 * 1024 * 1024

time: 34.4 us -> 34.1 us (level)
  no operation moved by 1% of the time
where the time goes in v3:
time: 34.1 us; the launch traced here: 33.9 us
  Pallas kernels  31.4 us (92%)
  local copies, waits for them, and re-layouts  2.5 us (7%)
    pallas_call x1, Pallas kernels, body(): pl.pallas_call(functools.partial(kernel, ring), out_shape=jax.ShapeDtypeS...  31.4 us
    unnamed x1, local copies, waits for them, and re-layouts  2.5 us

profile of v3, /device:TPU:1, one launch (start us, length us, event | category | flops | bytes accessed | tf_op | source)
XLA Modules:
  0.0 33.9 jit_solution(13256910863065227047)
XLA Ops:
  0.0 31.4 %shard_map.55 = f32[4,5,128,128]{3,2,1,0:T(8,128)} custom-call(f32[4,3,4,128,128]{4,3,2,1,0:T(8,128)} %ten_hbm.1, f32[4,5,128,128]{3,2,1,0:T(8,128)} %den_hbm.1, f32[4,4]{1,0:T(4,128)} %metric_hbm.1, s32[3,64]{1,0:T(4,128)} %bitcast.1, s32[64]{0:T(128)} %counts_hbm.1), custom_call_target="tpu_custom_call" | custom-call | flops 6000000000 | bytes 6000000 | tf_op jit(solution)/shard_map/pallas_call | solution.py:369
  31.4 2.5 %copy.7 = f32[4,5,128,128]{3,2,1,0:T(8,128)} copy(f32[4,5,128,128]{3,2,1,0:T(8,128)} %shard_map.55) | data formatting | bytes 2621440
